TPU v7x, 32 devices: a whole 2x2x4 slice. The times are simulated.
32 devices in a mesh: var: 8 (over y, x, core), head: 4 (over z).
Axes of the slice: x: 2, y: 2, z: 4, core: 2. Of those that a mesh axis runs over, the one named last changes fastest.
Arguments:
- queries: bfloat16 [4096, 8192], P('var', 'head'), may hold values from -5 to 5
- ablated: int32 [4096], P('var'), may hold values from 0 to 63
- head_keep: int32 [8, 64], P(None, 'head'), may hold values 0 or 1
- k_cache: bfloat16 [8, 2048, 1024], P('var', 'head'), may hold values from -4 to 4
- v_cache: bfloat16 [8, 2048, 1024], P('var', 'head'), may hold values from -40 to 40
- lengths: int32 [8], P('var'), may hold values from 512 to 2048, as said below
- out_weight: bfloat16 [8192, 4096], P('head', 'var'), may hold values from -0.09375 to 0.09375
- residual: bfloat16 [4096, 4096], P('var', 'head'), may hold values from -6 to 6
Outputs:
- patched: bfloat16 [4096, 4096], P('var', 'head')
Inputs may be any that keep to these rules, and one draw needn't show every extreme that they name: `lengths`: one prompt has exactly 2048 live positions.
All inputs are finite; a program needn't handle non-finite values. No bound on the sum of `head_keep` on one device may be relied on, other than what follows from the above.
Results may differ from a plain program's by a relative error of at most 0.012.
Values may be sent and summed in bfloat16 or wider, within the bound.
A program may use at most 192 MiB of HBM per device.

v0:
```python
import math

import jax
import jax.numpy as jnp
from jax import lax
from jax.sharding import PartitionSpec as P

HEADS = 64
KVH = 8
HD = 128


def attend(query_rows, full_keys, full_values, prompt_length):
    local_heads = query_rows.shape[1]
    group_size = HEADS // KVH
    score_scale = 1.0 / math.sqrt(HD)
    visible = jnp.arange(full_keys.shape[0]) < prompt_length
    pieces_out = []
    for column_pair in range(local_heads // 2):
        kv_index = 2 * column_pair // group_size
        query_pair = query_rows[:, 2 * column_pair : 2 * column_pair + 2, :]
        scores = (
            jnp.einsum(
                "rhd,td->hrt",
                query_pair,
                full_keys[:, kv_index, :],
                preferred_element_type=jnp.float32,
            )
            * score_scale
        )
        scores = jnp.where(visible, scores, -jnp.inf)
        row_max = jnp.max(scores, axis=-1, keepdims=True)
        exponent = jnp.exp(scores - row_max)
        probs = (exponent / jnp.sum(exponent, axis=-1, keepdims=True)).astype(jnp.bfloat16)
        outputs = jnp.einsum(
            "hrt,td->rhd", probs, full_values[:, kv_index, :], preferred_element_type=jnp.float32
        )
        pieces_out.append(outputs.astype(jnp.bfloat16))
    return jnp.concatenate(pieces_out, axis=1)


def project(gated, out_weight):
    partial_value = jnp.dot(
        gated,
        lax.all_gather(out_weight, "var", axis=1, tiled=True),
        preferred_element_type=jnp.float32,
    )
    return lax.psum_scatter(
        partial_value.astype(jnp.bfloat16), "head", scatter_dimension=1, tiled=True
    )


def per_device(queries, ablated, head_keep, k_cache, v_cache, lengths, out_weight, residual):
    row_count, feature_count = queries.shape
    var_count = lax.axis_size("var")
    head_count = lax.axis_size("head")
    local_heads = head_keep.shape[1]
    per_prompt = row_count // var_count
    head_position = lax.axis_index("head")
    copies = max(1, head_count // KVH)
    local_positions = k_cache.shape[1]
    stacked = jnp.stack([k_cache[0], v_cache[0]]).reshape(2, local_positions, KVH, HD)
    if copies > 1:
        stacked = jnp.repeat(stacked, copies, axis=2)
    arrived_kv = lax.all_to_all(stacked, "head", split_axis=2, concat_axis=1, tiled=True)
    full_keys = arrived_kv[0]
    full_values = arrived_kv[1]
    prompt_keep = jnp.repeat(head_keep, per_prompt, axis=0)
    heads_here = head_position * local_heads + jnp.arange(local_heads)
    kept_heads = jnp.where(ablated[:, None] != heads_here[None, :], prompt_keep, 0).astype(
        jnp.bfloat16
    )
    grouped = queries.reshape(var_count, per_prompt, feature_count)
    arrived, head_flags = (
        lax.all_to_all(grouped, "var", split_axis=0, concat_axis=0, tiled=True),
        lax.all_to_all(
            kept_heads.reshape(var_count, per_prompt, local_heads),
            "var",
            split_axis=0,
            concat_axis=0,
            tiled=True,
        ),
    )
    head_out = attend(
        arrived.reshape(row_count, local_heads, HD), full_keys, full_values, lengths[0]
    )
    gated = (head_out * head_flags.reshape(row_count, local_heads)[:, :, None]).reshape(
        row_count, feature_count
    )
    owner_rows = project(gated, out_weight)
    out_columns = owner_rows.shape[1]
    projected = lax.all_to_all(
        owner_rows.reshape(var_count, per_prompt, out_columns),
        "var",
        split_axis=0,
        concat_axis=0,
        tiled=True,
    ).reshape(row_count, out_columns)
    return (residual.astype(jnp.float32) + projected.astype(jnp.float32)).astype(jnp.bfloat16)


def solution(mesh):
    return jax.shard_map(
        per_device,
        mesh=mesh,
        in_specs=(
            P("var", "head"),
            P("var"),
            P(None, "head"),
            P("var", "head", None),
            P("var", "head", None),
            P("var"),
            P("head", "var"),
            P("var", "head"),
        ),
        out_specs=P("var", "head"),
        check_vma=False,
    )
```

profile of v0, /device:TPU:0, one launch (start us, length us, event | category | flops | bytes accessed | tf_op | source)
XLA Modules:
  0.0 318.8 jit_solution(8965007180376213215)
XLA Ops:
  8.9 9.7 %all_to_all.30 = bf16[8,2,512]{2,1,0:T(2,128)(2,1)S(1)} all-to-all(bf16[8,2,512]{2,1,0:T(2,128)(2,1)S(1)} %reshape.66), channel_id=1, replica_groups=mesh['var'=8,'head'=4] {'var'}, dimensions={0} | all-to-all | bytes 32768 | tf_op jit(solution)/shard_map/all_to_all | solution.py:76
  18.6 3.6 %all-to-all-start.1 = ((bf16[8,64,2048]{2,1,0:T(8,128)(2,1)}), bf16[8,64,2048]{2,1,0:T(8,128)(2,1)S(1)}, u32[]{:S(2)}, u32[]{:S(2)}) async-start(bf16[8,64,2048]{2,1,0:T(8,128)(2,1)} %bitcast.233), calls=%async_computation.1 | async-start | bytes 4194304 | tf_op jit(solution)/shard_map/all_to_all | solution.py:75
  23.8 2.3 copy.83
  29.1 40.4 %all-to-all-done.1 = bf16[8,64,2048]{2,1,0:T(8,128)(2,1)S(1)} async-done(((bf16[8,64,2048]{2,1,0:T(8,128)(2,1)}), bf16[8,64,2048]{2,1,0:T(8,128)(2,1)S(1)}, u32[]{:S(2)}, u32[]{:S(2)}) %all-to-all-start.1) | async-done | bytes 2097184 | tf_op jit(solution)/shard_map/all_to_all | solution.py:75
  70.8 4.6 %all-to-all-start = ((bf16[2,512,8,128]{1,3,0,2:T(8,128)(2,1)}), bf16[2,512,8,128]{1,3,0,2:T(8,128)(2,1)S(1)}, u32[]{:S(2)}, u32[]{:S(2)}) async-start(bf16[2,512,8,128]{1,3,0,2:T(8,128)(2,1)} %copy.84), calls=%async_computation | async-start | bytes 4194304 | tf_op jit(solution)/shard_map/all_to_all | solution.py:65
  76.3 2.3 copy.121
  78.6 2.5 fusion.185
  81.1 39.9 %all-to-all-done = bf16[2,512,8,128]{1,3,0,2:T(8,128)(2,1)S(1)} async-done(((bf16[2,512,8,128]{1,3,0,2:T(8,128)(2,1)}), bf16[2,512,8,128]{1,3,0,2:T(8,128)(2,1)S(1)}, u32[]{:S(2)}, u32[]{:S(2)}) %all-to-all-start) | async-done | bytes 2097184 | tf_op jit(solution)/shard_map/all_to_all | solution.py:65
  121.1 2.4 copy.85
  123.5 1.7 fusion.186
  127.2 7.0 %fusion.187 = (f32[2,512]{1,0:T(2,128)S(1)}, f32[2,512,2048]{1,2,0:T(8,128)}) fusion(pred[2048]{0:T(1024)(128)(4,1)S(1)} %iota_compare_fusion, bf16[512,2,128]{2,1,0:T(2,128)(2,1)} %get-tuple-element.12, bf16[2048,2,128]{2,0,1:T(8,128)(2,1)S(1)} %bitcast.235), kind=kOutput, calls=%fused_computation.174 | convolution fusion | flops 545261568 | bytes 9181184 | tf_op jit(solution)/shard_map/sub | solution.py:33
  134.2 6.0 %fusion.192 = (f32[2,512]{1,0:T(2,128)S(1)}, f32[2,512,2048]{1,2,0:T(8,128)}) fusion(pred[2048]{0:T(1024)(128)(4,1)S(1)} %iota_compare_fusion, bf16[512,2,128]{2,1,0:T(2,128)(2,1)S(1)} %copy-done.7, bf16[2048,2,128]{2,0,1:T(8,128)(2,1)S(1)} %bitcast.236), kind=kOutput, calls=%fused_computation.175 | convolution fusion | flops 545261568 | bytes 9181184 | tf_op jit(solution)/shard_map/sub | solution.py:33
  140.3 6.0 %fusion.197 = (f32[2,512]{1,0:T(2,128)S(1)}, f32[2,512,2048]{1,2,0:T(8,128)}) fusion(pred[2048]{0:T(1024)(128)(4,1)S(1)} %iota_compare_fusion, bf16[512,2,128]{2,1,0:T(2,128)(2,1)S(1)} %copy-done.6, bf16[2048,2,128]{2,0,1:T(8,128)(2,1)S(1)} %bitcast.237), kind=kOutput, calls=%fused_computation.176 | convolution fusion | flops 545261568 | bytes 9181184 | tf_op jit(solution)/shard_map/sub | solution.py:33
  146.3 6.0 %fusion.202 = (f32[2,512]{1,0:T(2,128)S(1)}, f32[2,512,2048]{1,2,0:T(8,128)}) fusion(pred[2048]{0:T(1024)(128)(4,1)S(1)} %iota_compare_fusion, bf16[512,2,128]{2,1,0:T(2,128)(2,1)S(1)} %copy-done.5, bf16[2048,2,128]{2,0,1:T(8,128)(2,1)S(1)} %bitcast.238), kind=kOutput, calls=%fused_computation.177 | convolution fusion | flops 545261568 | bytes 9181184 | tf_op jit(solution)/shard_map/sub | solution.py:33
  152.3 6.2 %fusion.207 = (f32[2,512]{1,0:T(2,128)S(1)}, f32[2,512,2048]{1,2,0:T(8,128)}) fusion(pred[2048]{0:T(1024)(128)(4,1)S(1)} %iota_compare_fusion, bf16[512,2,128]{2,1,0:T(2,128)(2,1)S(1)} %copy-done.4, bf16[2048,2,128]{2,0,1:T(8,128)(2,1)S(1)} %bitcast.239), kind=kOutput, calls=%fused_computation.178 | convolution fusion | flops 545261568 | bytes 9181184 | tf_op jit(solution)/shard_map/sub | solution.py:33
  158.6 6.0 %fusion.212 = (f32[2,512]{1,0:T(2,128)S(1)}, f32[2,512,2048]{1,2,0:T(8,128)}) fusion(pred[2048]{0:T(1024)(128)(4,1)S(1)} %iota_compare_fusion, bf16[512,2,128]{2,1,0:T(2,128)(2,1)S(1)} %copy-done.3, bf16[2048,2,128]{2,0,1:T(8,128)(2,1)S(1)} %bitcast.240), kind=kOutput, calls=%fused_computation.179 | convolution fusion | flops 545261568 | bytes 9181184 | tf_op jit(solution)/shard_map/sub | solution.py:33
  164.6 6.0 %fusion.217 = (f32[2,512]{1,0:T(2,128)S(1)}, f32[2,512,2048]{1,2,0:T(8,128)}) fusion(pred[2048]{0:T(1024)(128)(4,1)S(1)} %iota_compare_fusion, bf16[512,2,128]{2,1,0:T(2,128)(2,1)S(1)} %copy-done.2, bf16[2048,2,128]{2,0,1:T(8,128)(2,1)S(1)} %bitcast.241), kind=kOutput, calls=%fused_computation.180 | convolution fusion | flops 545261568 | bytes 9181184 | tf_op jit(solution)/shard_map/sub | solution.py:33
  170.6 6.1 %fusion.222 = (f32[2,512]{1,0:T(2,128)S(1)}, f32[2,512,2048]{1,2,0:T(8,128)}) fusion(pred[2048]{0:T(1024)(128)(4,1)S(1)} %iota_compare_fusion, bf16[512,2,128]{2,1,0:T(2,128)(2,1)S(1)} %get-tuple-element.5, bf16[2048,2,128]{2,0,1:T(8,128)(2,1)S(1)} %bitcast.242), kind=kOutput, calls=%fused_computation.181 | convolution fusion | flops 545261568 | bytes 9181184 | tf_op jit(solution)/shard_map/sub | solution.py:33
  176.7 4.1 %fusion.82 = bf16[512,16,128]{0,2,1:T(8,128)(2,1)S(1)} fusion(f32[2,512,2048]{1,2,0:T(8,128)} %get-tuple-element.16, f32[2,512]{1,0:T(2,128)S(1)} %get-tuple-element.15, bf16[2048,2,128]{0,2,1:T(8,128)(2,1)S(1)} %squeeze.14), kind=kOutput, calls=%fused_computation.101 | convolution fusion | flops 541196288 | bytes 9179136 | tf_op jit(solution)/shard_map/hrt,td->rhd/dot_general | solution.py:35
  180.9 4.3 %fusion.84 = bf16[512,16,128]{0,2,1:T(8,128)(2,1)S(1)} fusion(bf16[512,16,128]{0,2,1:T(8,128)(2,1)S(1)} %fusion.82, f32[2,512,2048]{1,2,0:T(8,128)} %get-tuple-element.18, f32[2,512]{1,0:T(2,128)S(1)} %get-tuple-element.17, bf16[2048,2,128]{0,2,1:T(8,128)(2,1)S(1)} %squeeze.14), kind=kOutput, calls=%fused_computation.103 | convolution fusion | flops 541196288 | bytes 9179136 | tf_op jit(solution)/shard_map/hrt,td->rhd/dot_general | solution.py:35
  185.1 4.3 %fusion.86 = bf16[512,16,128]{0,2,1:T(8,128)(2,1)S(1)} fusion(bf16[512,16,128]{0,2,1:T(8,128)(2,1)S(1)} %fusion.84, f32[2,512,2048]{1,2,0:T(8,128)} %get-tuple-element.20, f32[2,512]{1,0:T(2,128)S(1)} %get-tuple-element.19, bf16[2048,2,128]{0,2,1:T(8,128)(2,1)S(1)} %squeeze.14), kind=kOutput, calls=%fused_computation.105 | convolution fusion | flops 541196288 | bytes 9179136 | tf_op jit(solution)/shard_map/hrt,td->rhd/dot_general | solution.py:35
  200.7 14.0 %convolution_convert_fusion = bf16[512,4096]{1,0:T(8,128)(2,1)} fusion(bf16[512,2048]{0,1:T(8,128)(2,1)S(1)} %bitcast.234, bf16[2048,4096]{1,0:T(8,128)(2,1)} %all-gather.2.cloned.1.call-done), kind=kOutput, calls=%fused_computation.56 | convolution fusion | flops 8592031744 | bytes 23068672 | tf_op jit(solution)/shard_map/dot_general | solution.py:43
  214.7 76.4 %reduce-scatter.2.cloned.1.call-done = bf16[512,1024]{1,0:T(8,128)(2,1)} async-done(((bf16[512,4096]{1,0:T(8,128)(2,1)}), bf16[512,1024]{1,0:T(8,128)(2,1)}) %reduce-scatter.2.cloned.1.call-update) | async-done | bytes 1048592 | tf_op jit(solution)/shard_map/reduce_scatter | solution.py:48
  291.1 19.0 %all_to_all.31 = bf16[8,64,1024]{2,1,0:T(8,128)(2,1)S(1)} all-to-all(bf16[8,64,1024]{2,1,0:T(8,128)(2,1)} %bitcast.243), channel_id=1, replica_groups=mesh['var'=8,'head'=4] {'var'}, dimensions={0} | all-to-all | bytes 2097152 | tf_op jit(solution)/shard_map/all_to_all | solution.py:92
  (67 shorter events, 23.0 us)
Async XLA Ops:
  6.5 194.1 %all-gather.2.cloned.1.call-start = ((), (), s32[]{:S(2)}) async-start(), calls=%async_computation.5 | async-start | bytes 18874368 | tf_op jit(solution)/shard_map/all_gather | solution.py:45
  18.6 50.9 %all-to-all-start.1 = ((bf16[8,64,2048]{2,1,0:T(8,128)(2,1)}), bf16[8,64,2048]{2,1,0:T(8,128)(2,1)S(1)}, u32[]{:S(2)}, u32[]{:S(2)}) async-start(bf16[8,64,2048]{2,1,0:T(8,128)(2,1)} %bitcast.233), calls=%async_computation.1 | async-start | bytes 4194304 | tf_op jit(solution)/shard_map/all_to_all | solution.py:75
  69.5 1.3 copy-start
  70.8 50.3 %all-to-all-start = ((bf16[2,512,8,128]{1,3,0,2:T(8,128)(2,1)}), bf16[2,512,8,128]{1,3,0,2:T(8,128)(2,1)S(1)}, u32[]{:S(2)}, u32[]{:S(2)}) async-start(bf16[2,512,8,128]{1,3,0,2:T(8,128)(2,1)} %copy.84), calls=%async_computation | async-start | bytes 4194304 | tf_op jit(solution)/shard_map/all_to_all | solution.py:65
  75.4 215.7 %reduce-scatter.2.cloned.1.call-start = ((), (), s32[]{:S(2)}) async-start(), calls=%async_computation.6 | async-start | bytes 5242880 | tf_op jit(solution)/shard_map/reduce_scatter | solution.py:48
  127.2 7.1 %copy-start.7 = (bf16[512,2,128]{2,1,0:T(2,128)(2,1)S(1)}, bf16[512,2,128]{2,1,0:T(2,128)(2,1)}, u32[]{:S(2)}) copy-start(bf16[512,2,128]{2,1,0:T(2,128)(2,1)} %get-tuple-element.11) | copy-start | bytes 786436
  134.2 6.0 %copy-start.6 = (bf16[512,2,128]{2,1,0:T(2,128)(2,1)S(1)}, bf16[512,2,128]{2,1,0:T(2,128)(2,1)}, u32[]{:S(2)}) copy-start(bf16[512,2,128]{2,1,0:T(2,128)(2,1)} %get-tuple-element.10) | copy-start | bytes 786436
  140.3 6.0 %copy-start.5 = (bf16[512,2,128]{2,1,0:T(2,128)(2,1)S(1)}, bf16[512,2,128]{2,1,0:T(2,128)(2,1)}, u32[]{:S(2)}) copy-start(bf16[512,2,128]{2,1,0:T(2,128)(2,1)} %get-tuple-element.9) | copy-start | bytes 786436
  146.3 6.0 %copy-start.4 = (bf16[512,2,128]{2,1,0:T(2,128)(2,1)S(1)}, bf16[512,2,128]{2,1,0:T(2,128)(2,1)}, u32[]{:S(2)}) copy-start(bf16[512,2,128]{2,1,0:T(2,128)(2,1)} %get-tuple-element.8) | copy-start | bytes 786436
  152.3 6.2 %copy-start.3 = (bf16[512,2,128]{2,1,0:T(2,128)(2,1)S(1)}, bf16[512,2,128]{2,1,0:T(2,128)(2,1)}, u32[]{:S(2)}) copy-start(bf16[512,2,128]{2,1,0:T(2,128)(2,1)} %get-tuple-element.7) | copy-start | bytes 786436
  158.6 6.0 %copy-start.2 = (bf16[512,2,128]{2,1,0:T(2,128)(2,1)S(1)}, bf16[512,2,128]{2,1,0:T(2,128)(2,1)}, u32[]{:S(2)}) copy-start(bf16[512,2,128]{2,1,0:T(2,128)(2,1)} %get-tuple-element.6) | copy-start | bytes 786436
  180.8 8.6 %slice-start.8 = ((s8[8388608]{0:T(1024)(128)(4,1)}), s8[4194304]{0:T(1024)(128)(4,1)S(1)}, s32[]{:S(2)}) async-start(s8[8388608]{0:T(1024)(128)(4,1)} %bitcast.253), calls=%async_computation.15 | async-start | bytes 8388608
  185.1 4.6 %slice-start.9 = ((s8[8388608]{0:T(1024)(128)(4,1)}), s8[4194304]{0:T(1024)(128)(4,1)S(1)}, s32[]{:S(2)}) async-start(s8[8388608]{0:T(1024)(128)(4,1)} %bitcast.253), calls=%async_computation.16 | async-start | bytes 8388608
  185.1 5.8 %slice-start.6 = ((s8[8388608]{0:T(1024)(128)(4,1)}), s8[4194304]{0:T(1024)(128)(4,1)S(1)}, s32[]{:S(2)}) async-start(s8[8388608]{0:T(1024)(128)(4,1)} %bitcast.251), calls=%async_computation.13 | async-start | bytes 8388608
  189.8 2.6 slice-start.7
  189.8 3.8 %slice-start.4 = ((s8[8388608]{0:T(1024)(128)(4,1)}), s8[4194304]{0:T(1024)(128)(4,1)S(1)}, s32[]{:S(2)}) async-start(s8[8388608]{0:T(1024)(128)(4,1)} %bitcast.249), calls=%async_computation.11 | async-start | bytes 8388608
  192.3 2.4 slice-start.5
  192.3 3.6 %slice-start.2 = ((s8[8388608]{0:T(1024)(128)(4,1)}), s8[4194304]{0:T(1024)(128)(4,1)S(1)}, s32[]{:S(2)}) async-start(s8[8388608]{0:T(1024)(128)(4,1)} %bitcast.247), calls=%async_computation.9 | async-start | bytes 8388608
  194.8 2.4 slice-start.3
  194.8 3.6 %slice-start = ((s8[8388608]{0:T(1024)(128)(4,1)}), s8[4194304]{0:T(1024)(128)(4,1)S(1)}, s32[]{:S(2)}) async-start(s8[8388608]{0:T(1024)(128)(4,1)} %bitcast.245), calls=%async_computation.7 | async-start | bytes 8388608
  197.2 2.4 slice-start.1
  200.6 109.5 %copy-start.1 = (bf16[512,1024]{1,0:T(8,128)(2,1)S(1)}, bf16[512,1024]{1,0:T(8,128)(2,1)}, u32[]{:S(2)}) copy-start(bf16[512,1024]{1,0:T(8,128)(2,1)} %param.15) | copy-start | bytes 3145732
Sparse Core Ops, SparseCore 0:
  9.2 118.2 all-gather.1
  214.8 76.2 reduce-scatter.1
where the time goes:
time: 323 us; the launch traced here: 319 us
  waiting for transfers between devices  158 us (49%)
  matrix products  80.4 us (25%)
  blocking collectives  28.7 us (9%)
  local copies, waits for them, and re-layouts  25.4 us (8%)
  between operations  14.7 us (5%)
  starting transfers between devices  8.24 us (3%)
  other arithmetic  3.84 us (1%)
    reduce_scatter x1, waiting for transfers between devices, project(): lax.psum_scatter(partial_value.astype(jnp.bfloat16), 'head', scatter_dime...  76.4 us
    sub x8, matrix products, attend(): exponent = jnp.exp(scores - row_max)  49.5 us
    all_to_all x1, waiting for transfers between devices, per_device(): lax.all_to_all(grouped, 'var', split_axis=0, concat_axis=0, tiled=True)  40.4 us
    all_to_all x1, waiting for transfers between devices, per_device(): lax.all_to_all(stacked, 'head', split_axis=2, concat_axis=1, tiled=True)  39.9 us
    all_to_all x1, blocking collectives, per_device(): lax.all_to_all(owner_rows.reshape(var_count, per_prompt, out_columns), 'v...  19 us
    dot_general x8, matrix products, attend(): jnp.einsum('hrt,td->rhd', probs, full_values[:, kv_index, :], preferred_e...  16.9 us
    unnamed x41, local copies, waits for them, and re-layouts  14.3 us
    dot_general x1, matrix products, project(): jnp.dot(gated, lax.all_gather(out_weight, 'var', axis=1, tiled=True), pre...  14 us
  transfers between devices with their start and end apart: 4, of which 3 were waited for; matrix products, arithmetic and copies ran while one was open for 27% of the time, Pallas kernels for 0%

commit v1 on v0

v1 whole, which is shorter than its diff:
```python
import functools
import math

import jax
import jax.numpy as jnp
from jax import lax
from jax.experimental import pallas as pl
from jax.experimental.pallas import tpu as pltpu
from jax.sharding import PartitionSpec as P

HEADS = 64
KVH = 8
HD = 128
MESH = pl.DeviceIdType.MESH
DEAD = -1e30


def kernel(
    nv, nh, q_hbm, f_hbm, k_hbm, v_hbm, w_hbm, len_ref, res_ref, out_ref,
    qbuf, fbuf, qext, kbuf, vbuf, wbuf, gated, pbuf, rbuf, obuf, dbuf,
    q_send, q_recv, f_send, f_recv, kv_send, kv_recv, w_send, w_recv, x_send, x_recv,
    z_send, z_recv, o_send, o_recv, loc_sem,
):
    me_v, me_h = lax.axis_index("var"), lax.axis_index("head")
    rows, features = qbuf.shape
    per = rows // nv
    local_heads = features // HD
    group = HEADS // KVH
    kv_local = kbuf.shape[0]
    positions = k_hbm.shape[1]
    qcols = features // kv_local
    chips = nv // 2
    core = lax.rem(me_v, 2)
    chip = me_v // 2
    partner = me_v + 1 - 2 * core
    spd = nv // nh
    wcols = wbuf.shape[2]
    ocols = spd * wcols

    barrier = pltpu.get_barrier_semaphore()
    for i in range(1, nv):
        pl.semaphore_signal(barrier, inc=1, device_id=(lax.rem(me_v + i, nv), me_h), device_id_type=MESH)
    for i in range(1, nh):
        pl.semaphore_signal(barrier, inc=1, device_id=(me_v, lax.rem(me_h + i, nh)), device_id_type=MESH)
    pl.semaphore_wait(barrier, nv + nh - 2)

    def aligned(x, m):
        return pl.multiple_of(x * m, m)

    def q_copy(i, g):
        dst = lax.rem(me_v + i, nv)
        cols = pl.ds(g * qcols, qcols)
        return pltpu.make_async_remote_copy(
            q_hbm.at[pl.ds(aligned(dst, per), per), cols],
            qbuf.at[pl.ds(aligned(me_v, per), per), cols],
            q_send.at[g, i], q_recv.at[g, i], device_id=(dst, me_h), device_id_type=MESH)

    def f_copy(i):
        dst = lax.rem(me_v + i, nv)
        return pltpu.make_async_remote_copy(
            f_hbm.at[pl.ds(aligned(dst, per), per)],
            fbuf.at[pl.ds(aligned(me_v, per), per)],
            f_send.at[i], f_recv.at[i], device_id=(dst, me_h), device_id_type=MESH)

    def kv_refs(which, g, dst):
        src, buf = (k_hbm, kbuf) if which == 0 else (v_hbm, vbuf)
        start = (dst * local_heads) // group + g
        return (
            src.at[0, :, pl.ds(aligned(start, HD), HD)],
            buf.at[g, pl.ds(aligned(me_h, positions), positions), pl.ds(0, HD)],
        )

    def kv_copy(which, i, g):
        dst = lax.rem(me_h + i, nh)
        a, b = kv_refs(which, g, dst)
        return pltpu.make_async_remote_copy(
            a, b, kv_send.at[which, g, i], kv_recv.at[which, g, i],
            device_id=(me_v, dst), device_id_type=MESH)

    def w_copy(i):
        dst = lax.rem(chip + i, chips) * 2 + core
        return pltpu.make_async_remote_copy(
            w_hbm, wbuf.at[me_v], w_send.at[i], w_recv.at[i],
            device_id=(dst, me_h), device_id_type=MESH)

    def x_copy(i):
        slot = lax.rem(chip - i + chips, chips) * 2 + core
        return pltpu.make_async_remote_copy(
            w_hbm if i == 0 else wbuf.at[slot], wbuf.at[slot], x_send.at[i], x_recv.at[i],
            device_id=(partner, me_h), device_id_type=MESH)

    own = [
        pltpu.make_async_copy(
            q_hbm.at[pl.ds(aligned(me_v, per), per)], qbuf.at[pl.ds(aligned(me_v, per), per)], loc_sem.at[0]),
        pltpu.make_async_copy(
            f_hbm.at[pl.ds(aligned(me_v, per), per)], fbuf.at[pl.ds(aligned(me_v, per), per)], loc_sem.at[1]),
        pltpu.make_async_copy(w_hbm, wbuf.at[me_v], loc_sem.at[2]),
    ]
    for g in range(kv_local):
        for which in range(2):
            a, b = kv_refs(which, g, me_h)
            own.append(pltpu.make_async_copy(a, b, loc_sem.at[3 + 2 * g + which]))
    for g in range(kv_local):
        for which in range(2):
            for i in range(1, nh):
                kv_copy(which, i, g).start()
        for i in range(1, nv):
            q_copy(i, g).start()
        if g == 0:
            for i in range(1, nv):
                f_copy(i).start()
    for c in own:
        c.start()
    for i in range(1, chips):
        w_copy(i).start()
    x_copy(0).start()

    total = kbuf.shape[1]
    live = lax.broadcasted_iota(jnp.int32, (total, HD), 0) < len_ref[0]
    bias = jnp.where(live, 0.0, DEAD).astype(jnp.bfloat16)
    for g in range(kv_local):
        kbuf[g, :, HD:] = bias
        vbuf[g, :, HD:] = jnp.ones((total, HD), jnp.bfloat16)
    half = qext.shape[1]
    first = (lax.broadcasted_iota(jnp.int32, (half, HD), 1) == 0).astype(jnp.float32).astype(jnp.bfloat16)
    for b in range(qext.shape[0]):
        qext[b, :, HD:] = first

    for c in own:
        c.wait()
    for i in range(1, nv):
        f_copy(i).wait_recv()
    scale = math.log2(math.e) / math.sqrt(HD)
    heads_per = local_heads // kv_local
    for g in range(kv_local):
        for i in range(1, nv):
            q_copy(i, g).wait_recv()
        for which in range(2):
            for i in range(1, nh):
                kv_copy(which, i, g).wait_recv()

        def head_step(j, carry):
            head = g * heads_per + j
            cols = pl.ds(pl.multiple_of(head * HD, HD), HD)
            lane = lax.broadcasted_iota(jnp.int32, (half, HD), 1)
            for b in range(rows // half):
                here = pl.ds(b * half, half)
                qext[b, :, :HD] = qbuf[here, cols]
                scores = lax.dot_general(
                    qext[b], kbuf[g], (((1,), (1,)), ((), ())), preferred_element_type=jnp.float32)
                top = jnp.max(scores, axis=-1, keepdims=True)
                p = jnp.exp2((scores - top) * scale).astype(jnp.bfloat16)
                o = jnp.dot(p, vbuf[g], preferred_element_type=jnp.float32)
                result = (o[:, :HD] / o[:, HD:]).astype(jnp.bfloat16)
                flags = fbuf[here, :].astype(jnp.float32)
                keep = jnp.sum(jnp.where(lane == head, flags, 0.0), axis=-1, keepdims=True)
                gated[here, cols] = (result.astype(jnp.float32) * keep).astype(jnp.bfloat16)
            return carry

        lax.fori_loop(0, heads_per, head_step, 0)

    for i in range(1, chips):
        w_copy(i).wait_recv()
        x_copy(i).start()
    for i in range(chips):
        x_copy(i).wait_recv()

    def z_copy(i):
        dst = lax.rem(me_h + i, nh)
        return pltpu.make_async_remote_copy(
            pbuf.at[i], rbuf.at[i - 1], z_send.at[i], z_recv.at[i],
            device_id=(me_v, dst), device_id_type=MESH)

    for i in list(range(1, nh)) + [0]:
        dst = lax.rem(me_h + i, nh)

        def tile(t, carry):
            s, b = lax.rem(t, spd), t // spd
            here = pl.ds(pl.multiple_of(b * half, half), half)
            part = jnp.dot(gated[here, :], wbuf[dst * spd + s], preferred_element_type=jnp.float32)
            pbuf[i, here, pl.ds(pl.multiple_of(s * wcols, wcols), wcols)] = part.astype(jnp.bfloat16)
            return carry

        lax.fori_loop(0, spd * (rows // half), tile, 0)
        if i:
            z_copy(i).start()

    for i in range(1, nh):
        z_copy(i).wait_recv()

    def o_copy(dst):
        return pltpu.make_async_remote_copy(
            obuf.at[pl.ds(dst * per, per)], dbuf.at[pl.ds(aligned(me_v, per), per)],
            o_send.at[dst], o_recv.at[me_v], device_id=(dst, me_h), device_id_type=MESH)

    for dst in range(nv):
        here = pl.ds(dst * per, per)
        summed = pbuf[0, here, :].astype(jnp.float32)
        for i in range(1, nh):
            summed = summed + rbuf[i - 1, here, :].astype(jnp.float32)
        obuf[here, :] = summed.astype(jnp.bfloat16)

        @pl.when(dst != me_v)
        def _():
            o_copy(dst).start()

        @pl.when(dst == me_v)
        def _():
            dbuf[here, :] = obuf[here, :]

    for src in range(nv):
        here = pl.ds(src * per, per)

        @pl.when(src != me_v)
        def _():
            pltpu.make_async_remote_copy(
                obuf.at[here], dbuf.at[here], o_send.at[src], o_recv.at[src],
                device_id=(src, me_h), device_id_type=MESH).wait_recv()

        out_ref[here, :] = (
            res_ref[here, :].astype(jnp.float32) + dbuf[here, :].astype(jnp.float32)
        ).astype(jnp.bfloat16)

    for g in range(kv_local):
        for i in range(1, nv):
            q_copy(i, g).wait_send()
        for which in range(2):
            for i in range(1, nh):
                kv_copy(which, i, g).wait_send()
    for i in range(1, nv):
        f_copy(i).wait_send()
    for i in range(1, chips):
        w_copy(i).wait_send()
    for i in range(chips):
        x_copy(i).wait_send()
    for i in range(1, nh):
        z_copy(i).wait_send()
    for dst in range(nv):

        @pl.when(dst != me_v)
        def _():
            o_copy(dst).wait_send()


def per_device(queries, ablated, head_keep, k_cache, v_cache, lengths, out_weight, residual):
    rows, features = queries.shape
    nv, nh = lax.axis_size("var"), lax.axis_size("head")
    local_heads = head_keep.shape[1]
    per = rows // nv
    kv_local = max(1, KVH // nh)
    positions = k_cache.shape[1]
    total = positions * nh
    half = min(256, rows)
    wrows, wcols = out_weight.shape
    ocols = residual.shape[1]
    lane = jnp.arange(HD)
    keep = jnp.repeat(jnp.pad(head_keep, ((0, 0), (0, HD - local_heads))), per, axis=0)
    here = lax.axis_index("head") * local_heads + lane
    flags = jnp.where(ablated[:, None] != here[None, :], keep, 0).astype(jnp.bfloat16)
    any_spec = pl.BlockSpec(memory_space=pl.ANY)
    vmem = pl.BlockSpec(memory_space=pltpu.VMEM)
    bf16 = jnp.bfloat16
    dma = pltpu.SemaphoreType.DMA
    return pl.pallas_call(
        functools.partial(kernel, nv, nh),
        out_shape=jax.ShapeDtypeStruct((rows, ocols), bf16),
        in_specs=[any_spec] * 5 + [pl.BlockSpec(memory_space=pltpu.SMEM), vmem],
        out_specs=vmem,
        scratch_shapes=[
            pltpu.VMEM((rows, features), bf16),
            pltpu.VMEM((rows, HD), bf16),
            pltpu.VMEM((rows // half, half, 2 * HD), bf16),
            pltpu.VMEM((kv_local, total, 2 * HD), bf16),
            pltpu.VMEM((kv_local, total, 2 * HD), bf16),
            pltpu.VMEM((nv, wrows, wcols), bf16),
            pltpu.VMEM((rows, features), bf16),
            pltpu.VMEM((nh, rows, ocols), bf16),
            pltpu.VMEM((nh - 1, rows, ocols), bf16),
            pltpu.VMEM((rows, ocols), bf16),
            pltpu.VMEM((rows, ocols), bf16),
            dma((kv_local, nv)), dma((kv_local, nv)), dma((nv,)), dma((nv,)),
            dma((2, kv_local, nh)), dma((2, kv_local, nh)),
            dma((nv // 2,)), dma((nv // 2,)), dma((nv // 2,)), dma((nv // 2,)),
            dma((nh,)), dma((nh,)), dma((nv,)), dma((nv,)), dma((3 + 2 * kv_local,)),
        ],
        compiler_params=pltpu.CompilerParams(
            collective_id=0, has_side_effects=True, vmem_limit_bytes=60 * 1024 * 1024),
    )(queries, flags, k_cache, v_cache, out_weight, lengths, residual)


def solution(mesh):
    return jax.shard_map(
        per_device,
        mesh=mesh,
        in_specs=(
            P("var", "head"),
            P("var"),
            P(None, "head"),
            P("var", "head", None),
            P("var", "head", None),
            P("var"),
            P("head", "var"),
            P("var", "head"),
        ),
        out_specs=P("var", "head"),
        check_vma=False,
    )
```

time: 323 us -> 243 us (0.75)
  the two profiles are of different devices: /device:TPU:0 before, /device:TPU:13 now
where the time goes in v1:
time: 243 us
  Pallas kernels  238 us (98%)
  local copies, waits for them, and re-layouts  2.96 us (1%)
    pallas_call x1, Pallas kernels, per_device(): pl.pallas_call(functools.partial(kernel, nv, nh), out_shape=jax.ShapeDtyp...  238 us

profile of v1, /device:TPU:13, one launch (start us, length us, event | category | flops | bytes accessed | tf_op | source)
XLA Modules:
  0.0 243.1 jit_solution(8176073585346345240)
XLA Ops:
  0.7 0.7 pad.4
  1.4 1.5 fusion.f_hbm
  2.8 238.0 %shard_map.82 = bf16[512,1024]{1,0:T(8,128)(2,1)} custom-call(bf16[512,2048]{1,0:T(8,128)(2,1)} %q_hbm.1, bf16[512,128]{1,0:T(8,128)(2,1)} %fusion.f_hbm, bf16[1,512,1024]{2,1,0:T(8,128)(2,1)} %k_hbm.1, bf16[1,512,1024]{2,1,0:T(8,128)(2,1)} %v_hbm.1, bf16[2048,512]{1,0:T(8,128)(2,1)} %w_hbm.1, s32[1]{0:T(128)S(6)} %copy.10.len_ref, bf16[512,1024]{1,0:T(8,128)(2,1)} %res_ref.1), custom_call_target="tpu_custom_call" | custom-call | tf_op jit(solution)/shard_map/pallas_call | solution.py:264
  240.9 2.3 copy.11
  (1 shorter events, 0.0 us)

commit v2 on v1

--- a/solution.py
+++ b/solution.py
@@ -18,7 +18,8 @@
 def kernel(
     nv, nh, q_hbm, f_hbm, k_hbm, v_hbm, w_hbm, len_ref, res_ref, out_ref,
     qbuf, fbuf, qext, kbuf, vbuf, wbuf, gated, pbuf, rbuf, obuf, dbuf,
-    q_send, q_recv, f_send, f_recv, kv_send, kv_recv, w_send, w_recv, x_send, x_recv,
+    q_send, q_recv, f_send, f_recv, kv_send, kv_recv, row_send, row_recv, col_send, col_recv,
+    fr_send, fr_recv, fc_send, fc_recv, x_send, x_recv,
     z_send, z_recv, o_send, o_recv, loc_sem,
 ):
     me_v, me_h = lax.axis_index("var"), lax.axis_index("head")
@@ -77,17 +78,49 @@
             a, b, kv_send.at[which, g, i], kv_recv.at[which, g, i],
             device_id=(me_v, dst), device_id_type=MESH)
 
-    def w_copy(i):
-        dst = lax.rem(chip + i, chips) * 2 + core
-        return pltpu.make_async_remote_copy(
-            w_hbm, wbuf.at[me_v], w_send.at[i], w_recv.at[i],
-            device_id=(dst, me_h), device_id_type=MESH)
-
-    def x_copy(i):
-        slot = lax.rem(chip - i + chips, chips) * 2 + core
-        return pltpu.make_async_remote_copy(
-            w_hbm if i == 0 else wbuf.at[slot], wbuf.at[slot], x_send.at[i], x_recv.at[i],
+    wide = row_send.shape[0]
+    tall = col_send.shape[0]
+    cy, cx = chip // wide, lax.rem(chip, wide)
+    depth = wbuf.shape[1] // 2
+
+    def chip_at(i, j):
+        return lax.rem(cy + i + tall, tall) * wide + lax.rem(cx + j + wide, wide)
+
+    def w_part(slot, t):
+        return wbuf.at[slot, pl.ds(t * depth, depth)]
+
+    def w_own(t):
+        return w_hbm.at[pl.ds(t * depth, depth)]
+
+    def row_copy(j, t):
+        return pltpu.make_async_remote_copy(
+            w_own(t), w_part(me_v, t), row_send.at[j, t], row_recv.at[j, t],
+            device_id=(chip_at(0, j) * 2 + core, me_h), device_id_type=MESH)
+
+    def col_copy(i, t):
+        return pltpu.make_async_remote_copy(
+            w_own(t), w_part(me_v, t), col_send.at[i, t], col_recv.at[i, t],
+            device_id=(chip_at(i, 0) * 2 + core, me_h), device_id_type=MESH)
+
+    def forward_col(i, j):
+        part = w_part(chip_at(0, -j) * 2 + core, 0)
+        return pltpu.make_async_remote_copy(
+            part, part, fc_send.at[i, j], fc_recv.at[i, j],
+            device_id=(chip_at(i, 0) * 2 + core, me_h), device_id_type=MESH)
+
+    def forward_row(i, j):
+        part = w_part(chip_at(-i, 0) * 2 + core, 1)
+        return pltpu.make_async_remote_copy(
+            part, part, fr_send.at[i, j], fr_recv.at[i, j],
+            device_id=(chip_at(0, j) * 2 + core, me_h), device_id_type=MESH)
+
+    def x_copy(i, j, t):
+        part = w_part(chip_at(-i, -j) * 2 + core, t)
+        return pltpu.make_async_remote_copy(
+            w_own(t) if i == 0 and j == 0 else part, part, x_send.at[i, j, t], x_recv.at[i, j, t],
             device_id=(partner, me_h), device_id_type=MESH)
+
+    row_peers, col_peers = range(1, wide), range(1, tall)
 
     own = [
         pltpu.make_async_copy(
@@ -111,9 +144,13 @@
                 f_copy(i).start()
     for c in own:
         c.start()
-    for i in range(1, chips):
-        w_copy(i).start()
-    x_copy(0).start()
+    for t in range(2):
+        for j in row_peers:
+            row_copy(j, t).start()
+        for i in col_peers:
+            col_copy(i, 1 - t).start()
+    for t in range(2):
+        x_copy(0, 0, t).start()
 
     total = kbuf.shape[1]
     live = lax.broadcasted_iota(jnp.int32, (total, HD), 0) < len_ref[0]
@@ -158,35 +195,70 @@
             return carry
 
         lax.fori_loop(0, heads_per, head_step, 0)
-
-    for i in range(1, chips):
-        w_copy(i).wait_recv()
-        x_copy(i).start()
-    for i in range(chips):
-        x_copy(i).wait_recv()
-
-    def z_copy(i):
-        dst = lax.rem(me_h + i, nh)
-        return pltpu.make_async_remote_copy(
-            pbuf.at[i], rbuf.at[i - 1], z_send.at[i], z_recv.at[i],
+        if g == 0:
+            for j in row_peers:
+                row_copy(j, 0).wait_recv()
+                for i in col_peers:
+                    forward_col(i, j).start()
+                x_copy(0, j, 0).start()
+            for i in col_peers:
+                col_copy(i, 1).wait_recv()
+                for j in row_peers:
+                    forward_row(i, j).start()
+                x_copy(i, 0, 1).start()
+
+    blocks = rows // half
+
+    def z_copy(n, b, dst):
+        here = pl.ds(b * half, half)
+        return pltpu.make_async_remote_copy(
+            pbuf.at[n, here], rbuf.at[me_h, here], z_send.at[b, n], z_recv.at[b, me_h],
             device_id=(me_v, dst), device_id_type=MESH)
 
-    for i in list(range(1, nh)) + [0]:
-        dst = lax.rem(me_h + i, nh)
-
-        def tile(t, carry):
-            s, b = lax.rem(t, spd), t // spd
-            here = pl.ds(pl.multiple_of(b * half, half), half)
-            part = jnp.dot(gated[here, :], wbuf[dst * spd + s], preferred_element_type=jnp.float32)
-            pbuf[i, here, pl.ds(pl.multiple_of(s * wcols, wcols), wcols)] = part.astype(jnp.bfloat16)
-            return carry
-
-        lax.fori_loop(0, spd * (rows // half), tile, 0)
-        if i:
-            z_copy(i).start()
-
-    for i in range(1, nh):
-        z_copy(i).wait_recv()
+    def project(i, j):
+        n = i * wide + j
+        dst = chip_at(-i, -j)
+        for t in range(2):
+            x_copy(i, j, t).wait_recv()
+
+        for b in range(blocks):
+            here = pl.ds(b * half, half)
+
+            def tile(c, carry):
+                part = jnp.dot(gated[here, :], wbuf[dst * spd + c], preferred_element_type=jnp.float32)
+                pbuf[n, here, pl.ds(pl.multiple_of(c * wcols, wcols), wcols)] = part.astype(jnp.bfloat16)
+                return carry
+
+            lax.fori_loop(0, spd, tile, 0)
+
+            @pl.when(dst != me_h)
+            def _():
+                z_copy(n, b, dst).start()
+
+            @pl.when(dst == me_h)
+            def _():
+                rbuf[me_h, here, :] = pbuf[n, here, :]
+
+    project(0, 0)
+    for j in row_peers:
+        row_copy(j, 1).wait_recv()
+        x_copy(0, j, 1).start()
+    for i in col_peers:
+        col_copy(i, 0).wait_recv()
+        x_copy(i, 0, 0).start()
+    for j in row_peers:
+        project(0, j)
+    for i in col_peers:
+        project(i, 0)
+    for i in col_peers:
+        for j in row_peers:
+            forward_col(i, j).wait_recv()
+            x_copy(i, j, 0).start()
+            forward_row(i, j).wait_recv()
+            x_copy(i, j, 1).start()
+    for i in col_peers:
+        for j in row_peers:
+            project(i, j)
 
     def o_copy(dst):
         return pltpu.make_async_remote_copy(
@@ -195,9 +267,20 @@
 
     for dst in range(nv):
         here = pl.ds(dst * per, per)
-        summed = pbuf[0, here, :].astype(jnp.float32)
+        if dst * per % half == 0:
+            b = dst * per // half
+            lines = pl.ds(b * half, half)
+            for src in range(nh):
+
+                @pl.when(src != me_h)
+                def _():
+                    pltpu.make_async_remote_copy(
+                        pbuf.at[0, lines], rbuf.at[src, lines], z_send.at[b, 0], z_recv.at[b, src],
+                        device_id=(me_v, src), device_id_type=MESH).wait_recv()
+
+        summed = rbuf[0, here, :].astype(jnp.float32)
         for i in range(1, nh):
-            summed = summed + rbuf[i - 1, here, :].astype(jnp.float32)
+            summed = summed + rbuf[i, here, :].astype(jnp.float32)
         obuf[here, :] = summed.astype(jnp.bfloat16)
 
         @pl.when(dst != me_v)
@@ -229,12 +312,25 @@
                 kv_copy(which, i, g).wait_send()
     for i in range(1, nv):
         f_copy(i).wait_send()
-    for i in range(1, chips):
-        w_copy(i).wait_send()
-    for i in range(chips):
-        x_copy(i).wait_send()
-    for i in range(1, nh):
-        z_copy(i).wait_send()
+    for t in range(2):
+        for j in row_peers:
+            row_copy(j, t).wait_send()
+        for i in col_peers:
+            col_copy(i, t).wait_send()
+    for i in range(tall):
+        for j in range(wide):
+            if i and j:
+                forward_col(i, j).wait_send()
+                forward_row(i, j).wait_send()
+            for t in range(2):
+                x_copy(i, j, t).wait_send()
+            dst = chip_at(-i, -j)
+            for b in range(blocks):
+
+                @pl.when(dst != me_h)
+                def _():
+                    z_copy(i * wide + j, b, dst).wait_send()
+
     for dst in range(nv):
 
         @pl.when(dst != me_v)
@@ -253,6 +349,10 @@
     half = min(256, rows)
     wrows, wcols = out_weight.shape
     ocols = residual.shape[1]
+    chips = nv // 2
+    wide = max(d for d in range(1, chips + 1) if chips % d == 0 and d * d <= chips)
+    tall = chips // wide
+    blocks = rows // half
     lane = jnp.arange(HD)
     keep = jnp.repeat(jnp.pad(head_keep, ((0, 0), (0, HD - local_heads))), per, axis=0)
     here = lax.axis_index("head") * local_heads + lane
@@ -275,13 +375,15 @@
             pltpu.VMEM((nv, wrows, wcols), bf16),
             pltpu.VMEM((rows, features), bf16),
             pltpu.VMEM((nh, rows, ocols), bf16),
-            pltpu.VMEM((nh - 1, rows, ocols), bf16),
+            pltpu.VMEM((nh, rows, ocols), bf16),
             pltpu.VMEM((rows, ocols), bf16),
             pltpu.VMEM((rows, ocols), bf16),
             dma((kv_local, nv)), dma((kv_local, nv)), dma((nv,)), dma((nv,)),
             dma((2, kv_local, nh)), dma((2, kv_local, nh)),
-            dma((nv // 2,)), dma((nv // 2,)), dma((nv // 2,)), dma((nv // 2,)),
-            dma((nh,)), dma((nh,)), dma((nv,)), dma((nv,)), dma((3 + 2 * kv_local,)),
+            dma((wide, 2)), dma((wide, 2)), dma((tall, 2)), dma((tall, 2)),
+            dma((tall, wide)), dma((tall, wide)), dma((tall, wide)), dma((tall, wide)),
+            dma((tall, wide, 2)), dma((tall, wide, 2)),
+            dma((blocks, nh)), dma((blocks, nh)), dma((nv,)), dma((nv,)), dma((3 + 2 * kv_local,)),
         ],
         compiler_params=pltpu.CompilerParams(
             collective_id=0, has_side_effects=True, vmem_limit_bytes=60 * 1024 * 1024),

time: 243 us -> 189 us (0.78)
  the two profiles are of different devices: /device:TPU:13 before, /device:TPU:5 now
where the time goes in v2:
time: 189 us
  Pallas kernels  184 us (97%)
  local copies, waits for them, and re-layouts  2.96 us (2%)
    pallas_call x1, Pallas kernels, per_device(): pl.pallas_call(functools.partial(kernel, nv, nh), out_shape=jax.ShapeDtyp...  184 us

profile of v2, /device:TPU:5, one launch (start us, length us, event | category | flops | bytes accessed | tf_op | source)
XLA Modules:
  0.0 189.0 jit_solution(17296441045734416583)
XLA Ops:
  0.7 0.7 pad.4
  1.4 1.5 fusion.f_hbm
  2.8 183.9 %shard_map.82 = bf16[512,1024]{1,0:T(8,128)(2,1)} custom-call(bf16[512,2048]{1,0:T(8,128)(2,1)} %q_hbm.1, bf16[512,128]{1,0:T(8,128)(2,1)} %fusion.f_hbm, bf16[1,512,1024]{2,1,0:T(8,128)(2,1)} %k_hbm.1, bf16[1,512,1024]{2,1,0:T(8,128)(2,1)} %v_hbm.1, bf16[2048,512]{1,0:T(8,128)(2,1)} %w_hbm.1, s32[1]{0:T(128)S(6)} %copy.10.len_ref, bf16[512,1024]{1,0:T(8,128)(2,1)} %res_ref.1), custom_call_target="tpu_custom_call" | custom-call | tf_op jit(solution)/shard_map/pallas_call | solution.py:364
  186.7 2.3 %copy.11 = bf16[512,1024]{1,0:T(8,128)(2,1)} copy(bf16[512,1024]{1,0:T(8,128)(2,1)} %shard_map.82) | data formatting | bytes 2097152
  (1 shorter events, 0.0 us)

commit v3 on v2

--- a/solution.py
+++ b/solution.py
@@ -160,8 +160,8 @@
         vbuf[g, :, HD:] = jnp.ones((total, HD), jnp.bfloat16)
     half = qext.shape[1]
     first = (lax.broadcasted_iota(jnp.int32, (half, HD), 1) == 0).astype(jnp.float32).astype(jnp.bfloat16)
-    for b in range(qext.shape[0]):
-        qext[b, :, HD:] = first
+    for u in range(qext.shape[0]):
+        qext[u, :, HD:] = first
 
     for c in own:
         c.wait()
@@ -169,22 +169,19 @@
         f_copy(i).wait_recv()
     scale = math.log2(math.e) / math.sqrt(HD)
     heads_per = local_heads // kv_local
-    for g in range(kv_local):
-        for i in range(1, nv):
-            q_copy(i, g).wait_recv()
-        for which in range(2):
-            for i in range(1, nh):
-                kv_copy(which, i, g).wait_recv()
+    pair = 2 if heads_per % 2 == 0 else 1
+
+    def attend(g, b):
+        here = pl.ds(b * half, half)
 
         def head_step(j, carry):
-            head = g * heads_per + j
-            cols = pl.ds(pl.multiple_of(head * HD, HD), HD)
             lane = lax.broadcasted_iota(jnp.int32, (half, HD), 1)
-            for b in range(rows // half):
-                here = pl.ds(b * half, half)
-                qext[b, :, :HD] = qbuf[here, cols]
+            for u in range(pair):
+                head = g * heads_per + j * pair + u
+                cols = pl.ds(pl.multiple_of(head * HD, HD), HD)
+                qext[u, :, :HD] = qbuf[here, cols]
                 scores = lax.dot_general(
-                    qext[b], kbuf[g], (((1,), (1,)), ((), ())), preferred_element_type=jnp.float32)
+                    qext[u], kbuf[g], (((1,), (1,)), ((), ())), preferred_element_type=jnp.float32)
                 top = jnp.max(scores, axis=-1, keepdims=True)
                 p = jnp.exp2((scores - top) * scale).astype(jnp.bfloat16)
                 o = jnp.dot(p, vbuf[g], preferred_element_type=jnp.float32)
@@ -194,7 +191,46 @@
                 gated[here, cols] = (result.astype(jnp.float32) * keep).astype(jnp.bfloat16)
             return carry
 
-        lax.fori_loop(0, heads_per, head_step, 0)
+        lax.fori_loop(0, heads_per // pair, head_step, 0)
+
+    blocks = rows // half
+
+    def z_copy(n, b, dst):
+        here = pl.ds(b * half, half)
+        return pltpu.make_async_remote_copy(
+            pbuf.at[n, here], rbuf.at[me_h, here], z_send.at[b, n], z_recv.at[b, me_h],
+            device_id=(me_v, dst), device_id_type=MESH)
+
+    def project(i, j, b):
+        n = i * wide + j
+        dst = chip_at(-i, -j)
+        if b == 0:
+            for t in range(2):
+                x_copy(i, j, t).wait_recv()
+        here = pl.ds(b * half, half)
+
+        def tile(c, carry):
+            part = jnp.dot(gated[here, :], wbuf[dst * spd + c], preferred_element_type=jnp.float32)
+            pbuf[n, here, pl.ds(pl.multiple_of(c * wcols, wcols), wcols)] = part.astype(jnp.bfloat16)
+            return carry
+
+        lax.fori_loop(0, spd, tile, 0)
+
+        @pl.when(dst != me_h)
+        def _():
+            z_copy(n, b, dst).start()
+
+        @pl.when(dst == me_h)
+        def _():
+            rbuf[me_h, here, :] = pbuf[n, here, :]
+
+    for g in range(kv_local):
+        for i in range(1, nv):
+            q_copy(i, g).wait_recv()
+        for which in range(2):
+            for i in range(1, nh):
+                kv_copy(which, i, g).wait_recv()
+        attend(g, 0)
         if g == 0:
             for j in row_peers:
                 row_copy(j, 0).wait_recv()
@@ -207,58 +243,32 @@
                     forward_row(i, j).start()
                 x_copy(i, 0, 1).start()
 
-    blocks = rows // half
-
-    def z_copy(n, b, dst):
-        here = pl.ds(b * half, half)
-        return pltpu.make_async_remote_copy(
-            pbuf.at[n, here], rbuf.at[me_h, here], z_send.at[b, n], z_recv.at[b, me_h],
-            device_id=(me_v, dst), device_id_type=MESH)
-
-    def project(i, j):
-        n = i * wide + j
-        dst = chip_at(-i, -j)
-        for t in range(2):
-            x_copy(i, j, t).wait_recv()
-
-        for b in range(blocks):
-            here = pl.ds(b * half, half)
-
-            def tile(c, carry):
-                part = jnp.dot(gated[here, :], wbuf[dst * spd + c], preferred_element_type=jnp.float32)
-                pbuf[n, here, pl.ds(pl.multiple_of(c * wcols, wcols), wcols)] = part.astype(jnp.bfloat16)
-                return carry
-
-            lax.fori_loop(0, spd, tile, 0)
-
-            @pl.when(dst != me_h)
-            def _():
-                z_copy(n, b, dst).start()
-
-            @pl.when(dst == me_h)
-            def _():
-                rbuf[me_h, here, :] = pbuf[n, here, :]
-
-    project(0, 0)
+    near = [(0, j) for j in row_peers] + [(i, 0) for i in col_peers]
+    far = [(i, j) for i in col_peers for j in row_peers]
+    project(0, 0, 0)
     for j in row_peers:
         row_copy(j, 1).wait_recv()
         x_copy(0, j, 1).start()
     for i in col_peers:
         col_copy(i, 0).wait_recv()
         x_copy(i, 0, 0).start()
-    for j in row_peers:
-        project(0, j)
-    for i in col_peers:
-        project(i, 0)
-    for i in col_peers:
-        for j in row_peers:
-            forward_col(i, j).wait_recv()
-            x_copy(i, j, 0).start()
-            forward_row(i, j).wait_recv()
-            x_copy(i, j, 1).start()
-    for i in col_peers:
-        for j in row_peers:
-            project(i, j)
+    for i, j in near:
+        project(i, j, 0)
+    for b in range(1, blocks):
+        for g in range(kv_local):
+            attend(g, b)
+        project(0, 0, b)
+    for i, j in far:
+        forward_col(i, j).wait_recv()
+        x_copy(i, j, 0).start()
+        forward_row(i, j).wait_recv()
+        x_copy(i, j, 1).start()
+    for b in range(1, blocks):
+        for i, j in near:
+            project(i, j, b)
+    for b in range(blocks):
+        for i, j in far:
+            project(i, j, b)
 
     def o_copy(dst):
         return pltpu.make_async_remote_copy(
@@ -369,7 +379,7 @@
         scratch_shapes=[
             pltpu.VMEM((rows, features), bf16),
             pltpu.VMEM((rows, HD), bf16),
-            pltpu.VMEM((rows // half, half, 2 * HD), bf16),
+            pltpu.VMEM((2, half, 2 * HD), bf16),
             pltpu.VMEM((kv_local, total, 2 * HD), bf16),
             pltpu.VMEM((kv_local, total, 2 * HD), bf16),
             pltpu.VMEM((nv, wrows, wcols), bf16),

time: 189 us -> 188 us (level)
  no operation moved by 1% of the time
where the time goes in v3:
time: 188 us
  Pallas kernels  183 us (97%)
  local copies, waits for them, and re-layouts  2.96 us (2%)
    pallas_call x1, Pallas kernels, per_device(): pl.pallas_call(functools.partial(kernel, nv, nh), out_shape=jax.ShapeDtyp...  183 us

profile of v3, /device:TPU:5, one launch (start us, length us, event | category | flops | bytes accessed | tf_op | source)
XLA Modules:
  0.0 187.7 jit_solution(162704354707740512)
XLA Ops:
  0.7 0.7 pad.4
  1.4 1.5 fusion.f_hbm
  2.8 182.6 %shard_map.82 = bf16[512,1024]{1,0:T(8,128)(2,1)} custom-call(bf16[512,2048]{1,0:T(8,128)(2,1)} %q_hbm.1, bf16[512,128]{1,0:T(8,128)(2,1)} %fusion.f_hbm, bf16[1,512,1024]{2,1,0:T(8,128)(2,1)} %k_hbm.1, bf16[1,512,1024]{2,1,0:T(8,128)(2,1)} %v_hbm.1, bf16[2048,512]{1,0:T(8,128)(2,1)} %w_hbm.1, s32[1]{0:T(128)S(6)} %copy.10.len_ref, bf16[512,1024]{1,0:T(8,128)(2,1)} %res_ref.1), custom_call_target="tpu_custom_call" | custom-call | tf_op jit(solution)/shard_map/pallas_call | solution.py:374
  185.4 2.3 %copy.11 = bf16[512,1024]{1,0:T(8,128)(2,1)} copy(bf16[512,1024]{1,0:T(8,128)(2,1)} %shard_map.82) | data formatting | bytes 2097152
  (1 shorter events, 0.0 us)

commit v4 on v3

--- a/solution.py
+++ b/solution.py
@@ -142,13 +142,16 @@
         if g == 0:
             for i in range(1, nv):
                 f_copy(i).start()
+            for j in row_peers:
+                row_copy(j, 0).start()
+            for i in col_peers:
+                col_copy(i, 1).start()
     for c in own:
         c.start()
-    for t in range(2):
-        for j in row_peers:
-            row_copy(j, t).start()
-        for i in col_peers:
-            col_copy(i, 1 - t).start()
+    for j in row_peers:
+        row_copy(j, 1).start()
+    for i in col_peers:
+        col_copy(i, 0).start()
     for t in range(2):
         x_copy(0, 0, t).start()
 
@@ -258,14 +261,13 @@
         for g in range(kv_local):
             attend(g, b)
         project(0, 0, b)
+        for i, j in near:
+            project(i, j, b)
     for i, j in far:
         forward_col(i, j).wait_recv()
         x_copy(i, j, 0).start()
         forward_row(i, j).wait_recv()
         x_copy(i, j, 1).start()
-    for b in range(1, blocks):
-        for i, j in near:
-            project(i, j, b)
     for b in range(blocks):
         for i, j in far:
             project(i, j, b)

time: 188 us -> 188 us (level)
  no operation moved by 1% of the time
where the time goes in v4:
time: 188 us
  Pallas kernels  183 us (97%)
  local copies, waits for them, and re-layouts  2.96 us (2%)
    pallas_call x1, Pallas kernels, per_device(): pl.pallas_call(functools.partial(kernel, nv, nh), out_shape=jax.ShapeDtyp...  183 us

profile of v4, /device:TPU:5, one launch (start us, length us, event | category | flops | bytes accessed | tf_op | source)
XLA Modules:
  0.0 187.7 jit_solution(2710875689748777236)
XLA Ops:
  0.7 0.7 pad.4
  1.4 1.5 fusion.f_hbm
  2.8 182.6 %shard_map.82 = bf16[512,1024]{1,0:T(8,128)(2,1)} custom-call(bf16[512,2048]{1,0:T(8,128)(2,1)} %q_hbm.1, bf16[512,128]{1,0:T(8,128)(2,1)} %fusion.f_hbm, bf16[1,512,1024]{2,1,0:T(8,128)(2,1)} %k_hbm.1, bf16[1,512,1024]{2,1,0:T(8,128)(2,1)} %v_hbm.1, bf16[2048,512]{1,0:T(8,128)(2,1)} %w_hbm.1, s32[1]{0:T(128)S(6)} %copy.10.len_ref, bf16[512,1024]{1,0:T(8,128)(2,1)} %res_ref.1), custom_call_target="tpu_custom_call" | custom-call | tf_op jit(solution)/shard_map/pallas_call | solution.py:376
  185.4 2.3 %copy.11 = bf16[512,1024]{1,0:T(8,128)(2,1)} copy(bf16[512,1024]{1,0:T(8,128)(2,1)} %shard_map.82) | data formatting | bytes 2097152
  (1 shorter events, 0.0 us)
